TPU v7x, 32 devices: a whole 2x2x4 slice. The times are simulated.
32 devices in a mesh: lat: 8 (over z, y), lon: 4 (over x, core).
Axes of the slice: x: 2, y: 2, z: 4, core: 2. Of those that a mesh axis runs over, the one named last changes fastest.
Arguments:
- fields: float32 [2, 96, 24, 512], P(None, 'lat', 'lon'), may hold values from -13 to 13, as said below
- grad_out: float32 [2, 96, 24, 512], P(None, 'lat', 'lon'), may hold values from -6 to 6
- region_ids: int32 [2, 96, 24], P(None, 'lat', 'lon'), may hold values from 0 to 2
- bias_index: int32 [144, 144], replicated, may hold values from 0 to 6335
- bias_table: float32 [6336, 16], replicated, may hold values from -4 to 4
- in_weight: float32 [512, 1536], replicated, may hold values from -5 to 5, as said below
- out_weight: float32 [512, 512], replicated, may hold values from -0.25 to 0.25
Outputs:
- grad_fields: float32 [2, 96, 24, 512], P(None, 'lat', 'lon')
- grad_in_weight: float32 [512, 1536], P('lon')
- grad_out_weight: float32 [512, 512], P('lon')
- grad_bias: float32 [6336, 16], P('lon')
Inputs may be any that keep to these rules, and one draw needn't show every extreme that they name: `fields`: rows of the tokens have scales that differ widely. `in_weight`: Fan-in scaled; the query and key columns of each head carry a gain of their own.
All inputs are finite; a program needn't handle non-finite values.
Results may differ from a plain program's by a relative error of at most 0.0003.
Values sent between devices are 32-bit elements; how exact they have to be, the bound alone decides.
A program may use at most 128 MiB of HBM per device.

v0:
```python
import jax
import jax.numpy as jnp
from jax import lax
from jax.sharding import PartitionSpec as P

WIDTH = 512
HEADS = 16
HEAD_DIM = 32
WIN_LAT = 12
WIN_LON = 6


def shifted(value, axis, steps):
    count = lax.axis_size(axis)
    pairs = [(source, (source + steps) % count) for source in range(count)]
    return lax.ppermute(value, axis, pairs)


def extended(block, sides, width):
    for axis, dim in sides:
        count = lax.axis_size(axis)
        forward = [(i, i + 1) for i in range(count - 1)]
        backward = [(target, source) for source, target in forward]
        low = lax.ppermute(
            lax.slice_in_dim(block, block.shape[dim] - width, None, axis=dim), axis, forward
        )
        high = lax.ppermute(lax.slice_in_dim(block, 0, width, axis=dim), axis, backward)
        block = jnp.concatenate([low, block, high], axis=dim)
    return block


def split_windows(array):
    level_count, row_count, col_count = array.shape[:3]
    trailing = array.shape[3:]
    blocked = array.reshape(
        (level_count, row_count // WIN_LAT, WIN_LAT, col_count // WIN_LON, WIN_LON) + trailing
    )
    axis_order = (1, 3, 0, 2, 4) + tuple(range(5, 5 + len(trailing)))
    blocked = jnp.transpose(blocked, axis_order)
    return blocked.reshape(
        (row_count // WIN_LAT * (col_count // WIN_LON), level_count * WIN_LAT * WIN_LON) + trailing
    )


def join_windows(windows, level_count, row_count, col_count):
    trailing = windows.shape[2:]
    blocked = windows.reshape(
        (row_count // WIN_LAT, col_count // WIN_LON, level_count, WIN_LAT, WIN_LON) + trailing
    )
    axis_order = (2, 0, 3, 1, 4) + tuple(range(5, 5 + len(trailing)))
    blocked = jnp.transpose(blocked, axis_order)
    return blocked.reshape((level_count, row_count, col_count) + trailing)


def window_pass(inputs, cotangent, labels, owned, in_weight, out_weight, bias_full):
    highest = lax.Precision.HIGHEST
    average = jnp.mean(inputs, axis=-1, keepdims=True)
    centered = inputs - average
    variance = jnp.mean(centered * centered, axis=-1, keepdims=True)
    inv_std = lax.rsqrt(variance + 1e-05)
    normed = centered * inv_std
    projected = jnp.einsum("wtc,cf->wtf", normed, in_weight, precision=highest)
    win_count, tok_count = (inputs.shape[0], inputs.shape[1])
    heads_split = projected.reshape(win_count, tok_count, 3, HEADS, HEAD_DIM)
    queries = heads_split[:, :, 0]
    key_vecs = heads_split[:, :, 1]
    value_vecs = heads_split[:, :, 2]
    factor = HEAD_DIM ** (-0.5)
    scores = (
        jnp.einsum("wqhd,wkhd->whqk", queries, key_vecs, precision=highest) * factor
        + bias_full[None]
    )
    allowed = (labels[:, :, None] == labels[:, None, :]) & (labels[:, None, :] > 0.5)
    scores = jnp.where(allowed[:, None], scores, -1000000000.0)
    peak = jnp.max(scores, axis=-1, keepdims=True)
    exponent = jnp.exp(scores - peak)
    probs = exponent / jnp.sum(exponent, axis=-1, keepdims=True)
    attended = jnp.einsum("whqk,wkhd->wqhd", probs, value_vecs, precision=highest).reshape(
        win_count, tok_count, WIDTH
    )
    grad_attended = jnp.einsum("wte,ce->wtc", cotangent, out_weight, precision=highest)
    grad_out_part = jnp.einsum(
        "wtc,wte->ce", attended * owned[..., None], cotangent, precision=highest
    )
    grad_heads = grad_attended.reshape(win_count, tok_count, HEADS, HEAD_DIM)
    grad_probs = jnp.einsum("wqhd,wkhd->whqk", grad_heads, value_vecs, precision=highest)
    grad_values = jnp.einsum("whqk,wqhd->wkhd", probs, grad_heads, precision=highest)
    grad_scores = probs * (grad_probs - jnp.sum(grad_probs * probs, axis=-1, keepdims=True))
    grad_queries = jnp.einsum("whqk,wkhd->wqhd", grad_scores, key_vecs, precision=highest) * factor
    grad_keys = jnp.einsum("whqk,wqhd->wkhd", grad_scores, queries, precision=highest) * factor
    score_sum = jnp.einsum("whqk,wq->hqk", grad_scores, owned, precision=highest)
    grad_projected = jnp.stack([grad_queries, grad_keys, grad_values], axis=2).reshape(
        win_count, tok_count, 3 * WIDTH
    )
    grad_in_part = jnp.einsum(
        "wtc,wtf->cf", normed * owned[..., None], grad_projected, precision=highest
    )
    grad_normed = jnp.einsum("wtf,cf->wtc", grad_projected, in_weight, precision=highest)
    grad_inputs = inv_std * (
        grad_normed
        - jnp.mean(grad_normed, axis=-1, keepdims=True)
        - normed * jnp.mean(grad_normed * normed, axis=-1, keepdims=True)
    )
    return (grad_inputs, grad_in_part, grad_out_part, score_sum)


def sector_lookup(bias_table, bias_index, sector, table_rows, level_count):
    highest = lax.Precision.HIGHEST
    local_table = lax.dynamic_slice_in_dim(bias_table, sector * table_rows, table_rows, 0)
    local_index = (bias_index - sector * table_rows).reshape(level_count, -1)
    row_numbers = jnp.arange(table_rows, dtype=jnp.int32)
    pieces = []
    for level in range(level_count):
        one_hot = (row_numbers[:, None] == local_index[level][None, :]).astype(jnp.float32)
        pieces.append(jnp.dot(jnp.transpose(local_table), one_hot, precision=highest))
    return jnp.concatenate(pieces, axis=1)


def sector_scatter(score_total, bias_index, sector, table_rows, level_count):
    highest = lax.Precision.HIGHEST
    head_count = score_total.shape[0]
    flat_scores = score_total.reshape(head_count, level_count, -1)
    local_index = (bias_index - sector * table_rows).reshape(level_count, -1)
    row_numbers = jnp.arange(table_rows, dtype=jnp.int32)
    collected = jnp.zeros((head_count, table_rows), jnp.float32)
    for level in range(level_count):
        one_hot = (row_numbers[:, None] == local_index[level][None, :]).astype(jnp.float32)
        collected = collected + lax.dot_general(
            flat_scores[:, level], one_hot, (((1,), (1,)), ((), ())), precision=highest
        )
    return jnp.transpose(collected)


def body(fields, grad_out, region_ids, bias_index, bias_table, in_weight, out_weight):
    level_count, row_count, col_count, width = fields.shape
    half_rows = WIN_LAT // 2
    half_cols = WIN_LON // 2
    token_count = bias_index.shape[0]
    head_count = bias_table.shape[1]
    table_rows = bias_table.shape[0] // lax.axis_size("lon")
    sector = lax.axis_index("lon")
    labels = (region_ids + 1).astype(jnp.float32)
    looked_up = sector_lookup(bias_table, bias_index, sector, table_rows, level_count)
    bias_pairs = lax.psum(looked_up, "lon")
    bias_full = bias_pairs.reshape(head_count, token_count, token_count)
    strip_in, strip_grad, strip_labels = shifted(
        (fields[:, :, :half_cols], grad_out[:, :, :half_cols], labels[:, :, :half_cols]), "lon", -1
    )
    wide_in = jnp.concatenate([fields[:, :, half_cols:], strip_in], axis=2)
    wide_grad = jnp.concatenate([grad_out[:, :, half_cols:], strip_grad], axis=2)
    wide_labels = jnp.concatenate([labels[:, :, half_cols:], strip_labels], axis=2)
    first_col = 0
    ext_in, ext_grad, ext_labels = (
        extended(wide_in, (("lat", 1),), half_rows),
        extended(wide_grad, (("lat", 1),), half_rows),
        extended(wide_labels, (("lat", 1),), half_rows),
    )
    ext_rows = ext_in.shape[1]
    ext_cols = ext_in.shape[2]
    row_numbers = jnp.arange(ext_rows)
    col_numbers = jnp.arange(ext_cols)
    row_owned = (row_numbers >= half_rows) & (row_numbers < half_rows + row_count)
    col_owned = (col_numbers >= first_col) & (col_numbers < first_col + col_count)
    owned_grid = jnp.broadcast_to(
        (row_owned[:, None] & col_owned[None, :]).astype(jnp.float32),
        (level_count, ext_rows, ext_cols),
    )
    grad_win, grad_in_part, grad_out_part, score_sum = window_pass(
        split_windows(ext_in),
        split_windows(ext_grad),
        split_windows(ext_labels),
        split_windows(owned_grid),
        in_weight,
        out_weight,
        bias_full,
    )
    grad_ext = join_windows(grad_win, level_count, ext_rows, ext_cols)
    own_block = grad_ext[:, half_rows : half_rows + row_count, first_col : first_col + col_count]
    returned = shifted(own_block[:, :, col_count - half_cols :], "lon", 1)
    grad_attn = jnp.concatenate([returned, own_block[:, :, : col_count - half_cols]], axis=2)
    grad_fields = grad_out + grad_attn
    full_in, full_out, score_total = lax.psum(
        (grad_in_part, grad_out_part, score_sum), ("lat", "lon")
    )
    block_rows = width // lax.axis_size("lon")
    grad_in_weight = lax.dynamic_slice_in_dim(full_in, sector * block_rows, block_rows, 0)
    grad_out_weight = lax.dynamic_slice_in_dim(full_out, sector * block_rows, block_rows, 0)
    grad_bias = sector_scatter(score_total, bias_index, sector, table_rows, level_count)
    return (grad_fields, grad_in_weight, grad_out_weight, grad_bias)


def solution(mesh):
    in_specs = (
        P(None, "lat", "lon", None),
        P(None, "lat", "lon", None),
        P(None, "lat", "lon"),
        P(),
        P(),
        P(),
        P(),
    )
    out_specs = (P(None, "lat", "lon", None), P("lon", None), P("lon", None), P("lon", None))
    return jax.shard_map(body, mesh=mesh, in_specs=in_specs, out_specs=out_specs, check_vma=False)
```

profile of v0, /device:TPU:0, one launch (start us, length us, event | category | flops | bytes accessed | tf_op | source)
XLA Modules:
  0.0 406.7 jit_solution(11198453574197482551)
XLA Ops:
  15.4 21.4 %fusion.1 = f32[16,10368]{1,0:T(8,128)S(1)} fusion(s32[10368]{0:T(1024)S(1)} %eq.72, f32[6336,16]{0,1:T(8,128)} %param.11, s32[]{:T(128)S(6)} %select_n.11), kind=kOutput, calls=%fused_computation.2 | convolution fusion | flops 3169622016 | bytes 811524 | tf_op jit(solution)/shard_map/dot_general | solution.py:115
  36.8 21.9 %fusion.3 = f32[16,10368]{1,0:T(8,128)S(1)} fusion(s32[10368]{0:T(1024)S(1)} %eq.33, f32[6336,16]{0,1:T(8,128)} %param.11, s32[]{:T(128)S(6)} %select_n.11), kind=kOutput, calls=%fused_computation.5 | convolution fusion | flops 3169622016 | bytes 811524 | tf_op jit(solution)/shard_map/dot_general | solution.py:115
  59.8 3.1 add.58
  68.7 4.5 %collective-permute-start.4 = (f32[2,6,6]{1,0,2:T(2,128)S(1)}, f32[2,6,6]{1,0,2:T(2,128)S(1)}, u32[]{:S(2)}, u32[]{:S(2)}) collective-permute-start(f32[2,6,6]{1,0,2:T(2,128)S(1)} %get-tuple-element.27), channel_id=1, source_target_pairs={{0,4},{4,8},{8,12},{12,16},{16,20},{20,24},{24,28},{1,5},{5,9},{9,... | collective-permute-start | bytes 872 | tf_op jit(solution)/shard_map/ppermute | solution.py:24
  73.3 3.5 copy.64
  79.7 5.0 %collective-permute-start.1 = (f32[2,6,6,512]{3,0,2,1:T(2,128)S(1)}, f32[2,6,6,512]{3,0,2,1:T(2,128)S(1)}, u32[]{:S(2)}, u32[]{:S(2)}) collective-permute-start(f32[2,6,6,512]{3,0,2,1:T(2,128)S(1)} %get-tuple-element.17), channel_id=1, source_target_pairs={{0,4},{4,8},{8,12},{12,16},{16,20},{20,24},{24,28},{1,5},{5,9},{9,... | collective-permute-start | bytes 442376 | tf_op jit(solution)/shard_map/ppermute | solution.py:24
  87.2 5.6 %collective-permute-start.7 = (f32[2,6,6,512]{3,0,2,1:T(2,128)S(1)}, f32[2,6,6,512]{3,0,2,1:T(2,128)S(1)}, u32[]{:S(2)}, u32[]{:S(2)}) collective-permute-start(f32[2,6,6,512]{3,0,2,1:T(2,128)S(1)} %get-tuple-element.21), channel_id=1, source_target_pairs={{0,4},{4,8},{8,12},{12,16},{16,20},{20,24},{24,28},{1,5},{5,9},{9,... | collective-permute-start | bytes 442376 | tf_op jit(solution)/shard_map/ppermute | solution.py:24
  95.3 3.2 collective-permute-done.7
  106.6 7.0 %fusion.25 = f32[2,144,3,16,32]{1,4,3,2,0:T(8,128)S(1)} fusion(f32[3,16,32,512,1]{3,2,1,0,4:T(8,128)} %bitcast.102, f32[2,144,512,1,1]{2,0,1,4,3:T(2,128)S(1)} %bitcast.114), kind=kOutput, calls=%fused_computation.44 | convolution fusion | flops 2717908992 | bytes 5505024 | tf_op jit(solution)/shard_map/wtc,cf->wtf/dot_general | solution.py:62
  113.6 7.8 %all-reduce.4.cloned.1.call-done = f32[16,144,144]{1,2,0:T(8,128)} async-done(((f32[16,144,144]{1,2,0:T(8,128)}), f32[16,144,144]{1,2,0:T(8,128)}) %all-reduce.4.cloned.1.call-update) | async-done | bytes 1327120 | tf_op jit(solution)/shard_map/psum | solution.py:144
  121.4 7.2 %fusion.12 = (f32[2,16,144]{2,1,0:T(8,128)S(1)}, f32[2,16,144,144]{2,3,1,0:T(8,128)S(1)}) fusion(f32[16,144,144]{1,2,0:T(8,128)} %all-reduce.4.cloned.1.call-done, pred[2,144,144]{1,2,0:T(8,128)(4,1)S(1)} %compare_and_fusion, f32[2,144,3,16,32]{1,4,3,2,0:T(8,128)S(1)} %fusion.25), kind=kOutput, calls=%fused_computation.21 | convolution fusion | flops 257453568 | bytes 6170624 | tf_op jit(solution)/shard_map/wqhd,wkhd->whqk/dot_general | solution.py:70
  130.0 6.0 %multiply_reduce_fusion.1 = (f32[2,16,144]{2,1,0:T(8,128)S(1)}, f32[2,16,144,144]{2,3,1,0:T(8,128)S(1)}, f32[2,16,144,144]{2,3,1,0:T(8,128)S(1)}) fusion(f32[2,16,144]{2,1,0:T(8,128)S(1)} %fusion.9, f32[2,16,144]{2,1,0:T(8,128)S(1)} %get-tuple-element.31, f32[16,144,144]{1,2,0:T(8,128)S(1)} %copy-done.3, f32[2,16,144,144]{2,3,1,0:T(8,128)S(1)} %get-tuple-element.32, ...), kind=kOutput, calls=%fused_computation.12 | convolution fusion | flops 259444224 | bytes 14641152 | tf_op jit(solution)/shard_map/wqhd,wkhd->whqk/dot_general | solution.py:86
  136.0 5.0 %convolution_bitcast_fusion.2 = f32[2,144,1,16,32]{1,4,3,0,2:T(8,128)S(1)} fusion(f32[2,144,16,32]{1,3,2,0:T(8,128)S(1)} %copy-done.4, f32[2,16,144,144]{2,3,1,0:T(8,128)S(1)} %get-tuple-element.12), kind=kOutput, calls=%fused_computation.24 | convolution fusion | flops 254803968 | bytes 3833856 | tf_op jit(solution)/shard_map/whqk,wqhd->wkhd/dot_general | solution.py:87
  143.7 4.5 %fusion.14 = f32[2,144,1,16,32]{1,4,3,0,2:T(8,128)S(1)} fusion(f32[2,16,144,144]{2,3,1,0:T(8,128)S(1)} %get-tuple-element.10, f32[2,144,3,16,32]{1,4,3,2,0:T(8,128)S(1)} %fusion.25), kind=kOutput, calls=%fused_computation.26 | convolution fusion | flops 254951424 | bytes 6356992 | tf_op jit(solution)/shard_map/whqk,wqhd->wkhd/dot_general | solution.py:90
  150.9 3.8 fusion.17
  157.8 3.5 copy.97
  161.2 4.1 %reshape.140 = f32[16,2,10368]{2,1,0:T(2,128)} reshape(f32[16,144,144]{2,1,0:T(8,128)} %bitcast.110) | data formatting | bytes 2654208 | tf_op jit(solution)/shard_map/reshape | solution.py:122
  165.4 4.2 %convolution_bitcast_fusion.1 = f32[512,512]{1,0:T(8,128)} fusion(f32[2,144,512]{2,0,1:T(2,128)} %bitcast.112, f32[2,144,512]{2,1,0:T(8,128)} %copy.81, f32[2,144]{1,0:T(2,128)S(1)} %transpose.74), kind=kOutput, calls=%fused_computation.23 | convolution fusion | flops 906117120 | bytes 2229376 | tf_op jit(solution)/shard_map/wtc,wte->ce/dot_general | solution.py:82
  169.5 12.9 %convolution_bitcast_fusion = f32[512,1536]{1,0:T(8,128)} fusion(f32[2,144,1536]{1,2,0:T(8,128)S(1)} %bitcast.100, f32[2,144,512]{2,0,1:T(2,128)} %bitcast.107, f32[2,144]{1,0:T(2,128)S(1)} %transpose.74, f32[2,144]{1,0:T(2,128)S(1)} %div.27, f32[2,144]{1,0:T(2,128)S(1)} %rsqrt.13), kind=kOutput, calls=%fused_computation.17 | convolution fusion | flops 2718351360 | bytes 5508480 | tf_op jit(solution)/shard_map/wtc,wtf->cf/dot_general | solution.py:95
  182.5 12.6 %fusion.43 = (f32[2,144]{1,0:T(2,128)S(1)}, f32[2,144]{1,0:T(2,128)S(1)}, f32[2,144,512]{2,1,0:T(8,128)S(1)}) fusion(f32[2,144]{1,0:T(2,128)S(1)} %rsqrt.13, f32[2,144]{1,0:T(2,128)S(1)} %div.27, f32[2,144,512]{2,0,1:T(2,128)} %bitcast.108, f32[2,144,1536]{1,2,0:T(8,128)S(1)} %bitcast.101, f32[512,1536]{1,0:T(8,128)} %param.12), kind=kOutput, calls=%fused_computation.90 | convolution fusion | flops 2718645760 | bytes 6099456 | tf_op jit(solution)/shard_map/wtf,cf->wtc/dot_general | solution.py:98
  196.4 4.6 %collective-permute-done.9 = f32[2,12,3,512]{3,0,2,1:T(2,128)S(1)} collective-permute-done((f32[2,12,3,512]{3,0,2,1:T(2,128)S(1)}, f32[2,12,3,512]{3,0,2,1:T(2,128)S(1)}, u32[]{:S(2)}, u32[]{:S(2)}) %collective-permute-start.9) | collective-permute-done | bytes 147488 | tf_op jit(solution)/shard_map/ppermute | solution.py:16
  201.9 131.7 %all-reduce.6.cloned.1.call-done = (f32[512,1536]{1,0:T(8,128)}, f32[512,512]{1,0:T(8,128)}, f32[16,2,10368]{2,1,0:T(2,128)}) async-done(((f32[512,1536]{1,0:T(8,128)}, f32[512,512]{1,0:T(8,128)}, f32[16,2,10368]{2,1,0:T(2,128)}), (f32[512,1536]{1,0:T(8,128)}, f32[512,512]{1,0:T(8,128)}, f32[16,2,10368]{2,1,0:T(2,128)})) %all-reduce.6.cloned.1.call-update) | async-done | bytes 5521424 | tf_op jit(solution)/shard_map/psum | solution.py:182
  340.4 29.4 %fusion = f32[1584,16]{0,1:T(8,128)S(1)} fusion(s32[10368]{0:T(1024)S(1)} %copy-done.9, f32[16,1,10368]{2,1,0:T(1,128)S(1)} %get-tuple-element.14), kind=kOutput, calls=%fused_computation.1 | convolution fusion | flops 3169622016 | bytes 806400 | tf_op jit(solution)/shard_map/dot_general | solution.py:128
  369.9 29.8 %fusion.13 = f32[1584,16]{0,1:T(8,128)} fusion(f32[1584,16]{0,1:T(8,128)S(1)} %fusion, s32[10368]{0:T(1024)S(1)} %copy-done.11, f32[16,1,10368]{2,1,0:T(1,128)S(1)} %get-tuple-element.13), kind=kOutput, calls=%fused_computation.22 | convolution fusion | flops 3169647360 | bytes 907776 | tf_op jit(solution)/shard_map/dot_general | solution.py:128
  (96 shorter events, 49.7 us)
Async XLA Ops:
  7.2 93.0 %copy-start = (f32[512,512]{1,0:T(8,128)S(1)}, f32[512,512]{1,0:T(8,128)}, u32[]{:S(2)}) copy-start(f32[512,512]{1,0:T(8,128)} %param.13) | copy-start | bytes 3145732
  7.2 114.2 %all-reduce.4.cloned.1.call-start = ((), (), s32[]{:S(2)}) async-start(), calls=%async_computation | async-start | bytes 4718592 | tf_op jit(solution)/shard_map/psum | solution.py:144
  9.0 68.3 %collective-permute-start = (f32[2,12,3,512]{3,0,2,1:T(2,128)}, f32[2,12,3,512]{3,0,2,1:T(2,128)}, u32[]{:S(2)}, u32[]{:S(2)}) collective-permute-start(f32[2,12,3,512]{3,0,2,1:T(2,128)} %get-tuple-element.20), channel_id=1, source_target_pairs={{0,3},{1,0},{2,1},{3,2},{4,7},{5,4},{6,5},{7,6},{8,11},{9,8},{10,9... | collective-permute-start | bytes 442376 | tf_op jit(solution)/shard_map/ppermute | solution.py:16
  13.1 71.8 %collective-permute-start.6 = (f32[2,12,3,512]{3,0,2,1:T(2,128)}, f32[2,12,3,512]{3,0,2,1:T(2,128)}, u32[]{:S(2)}, u32[]{:S(2)}) collective-permute-start(f32[2,12,3,512]{3,0,2,1:T(2,128)} %get-tuple-element.24), channel_id=1, source_target_pairs={{0,3},{1,0},{2,1},{3,2},{4,7},{5,4},{6,5},{7,6},{8,11},{9,8},{10,9... | collective-permute-start | bytes 442376 | tf_op jit(solution)/shard_map/ppermute | solution.py:16
  14.8 0.6 copy-start.8
  14.9 21.9 %copy-start.10 = (s32[10368]{0:T(1024)}, s32[10368]{0:T(1024)S(1)}, u32[]{:S(2)}) copy-start(s32[10368]{0:T(1024)S(1)} %eq.33) | copy-start | bytes 124420
  65.2 12.1 %copy-start.6 = (f32[2,12,3,512]{3,0,2,1:T(2,128)S(1)}, f32[2,12,3,512]{3,0,2,1:T(2,128)}, u32[]{:S(2)}) copy-start(f32[2,12,3,512]{3,0,2,1:T(2,128)} %get-tuple-element.19) | copy-start | bytes 442372
  65.3 268.4 %all-reduce.6.cloned.1.call-start = ((), (), s32[]{:S(2)}) async-start(), calls=%async_computation.1 | async-start | bytes 11042816 | tf_op jit(solution)/shard_map/psum | solution.py:182
  66.0 1.3 collective-permute-start.3
  67.4 9.5 %collective-permute-start.5 = (f32[2,6,6]{1,0,2:T(2,128)S(1)}, f32[2,6,6]{1,0,2:T(2,128)S(1)}, u32[]{:S(2)}, u32[]{:S(2)}) collective-permute-start(f32[2,6,6]{1,0,2:T(2,128)S(1)} %get-tuple-element.28), channel_id=1, source_target_pairs={{4,0},{8,4},{12,8},{16,12},{20,16},{24,20},{28,24},{5,1},{9,5},{13... | collective-permute-start | bytes 872 | tf_op jit(solution)/shard_map/ppermute | solution.py:27
  68.7 8.2 %collective-permute-start.4 = (f32[2,6,6]{1,0,2:T(2,128)S(1)}, f32[2,6,6]{1,0,2:T(2,128)S(1)}, u32[]{:S(2)}, u32[]{:S(2)}) collective-permute-start(f32[2,6,6]{1,0,2:T(2,128)S(1)} %get-tuple-element.27), channel_id=1, source_target_pairs={{0,4},{4,8},{8,12},{12,16},{16,20},{20,24},{24,28},{1,5},{5,9},{9,... | collective-permute-start | bytes 872 | tf_op jit(solution)/shard_map/ppermute | solution.py:24
  78.4 14.4 %collective-permute-start.2 = (f32[2,6,6,512]{3,0,2,1:T(2,128)S(1)}, f32[2,6,6,512]{3,0,2,1:T(2,128)S(1)}, u32[]{:S(2)}, u32[]{:S(2)}) collective-permute-start(f32[2,6,6,512]{3,0,2,1:T(2,128)S(1)} %get-tuple-element.18), channel_id=1, source_target_pairs={{4,0},{8,4},{12,8},{16,12},{20,16},{24,20},{28,24},{5,1},{9,5},{13... | collective-permute-start | bytes 442376 | tf_op jit(solution)/shard_map/ppermute | solution.py:27
  79.7 13.1 %collective-permute-start.1 = (f32[2,6,6,512]{3,0,2,1:T(2,128)S(1)}, f32[2,6,6,512]{3,0,2,1:T(2,128)S(1)}, u32[]{:S(2)}, u32[]{:S(2)}) collective-permute-start(f32[2,6,6,512]{3,0,2,1:T(2,128)S(1)} %get-tuple-element.17), channel_id=1, source_target_pairs={{0,4},{4,8},{8,12},{12,16},{16,20},{20,24},{24,28},{1,5},{5,9},{9,... | collective-permute-start | bytes 442376 | tf_op jit(solution)/shard_map/ppermute | solution.py:24
  85.9 9.4 %collective-permute-start.8 = (f32[2,6,6,512]{3,0,2,1:T(2,128)S(1)}, f32[2,6,6,512]{3,0,2,1:T(2,128)S(1)}, u32[]{:S(2)}, u32[]{:S(2)}) collective-permute-start(f32[2,6,6,512]{3,0,2,1:T(2,128)S(1)} %get-tuple-element.22), channel_id=1, source_target_pairs={{4,0},{8,4},{12,8},{16,12},{20,16},{24,20},{28,24},{5,1},{9,5},{13... | collective-permute-start | bytes 442376 | tf_op jit(solution)/shard_map/ppermute | solution.py:27
  87.2 11.3 %collective-permute-start.7 = (f32[2,6,6,512]{3,0,2,1:T(2,128)S(1)}, f32[2,6,6,512]{3,0,2,1:T(2,128)S(1)}, u32[]{:S(2)}, u32[]{:S(2)}) collective-permute-start(f32[2,6,6,512]{3,0,2,1:T(2,128)S(1)} %get-tuple-element.21), channel_id=1, source_target_pairs={{0,4},{4,8},{8,12},{12,16},{16,20},{20,24},{24,28},{1,5},{5,9},{9,... | collective-permute-start | bytes 442376 | tf_op jit(solution)/shard_map/ppermute | solution.py:24
  100.2 0.8 copy-start.5
  121.4 7.2 %copy-start.3 = (f32[16,144,144]{1,2,0:T(8,128)S(1)}, f32[16,144,144]{1,2,0:T(8,128)}, u32[]{:S(2)}) copy-start(f32[16,144,144]{1,2,0:T(8,128)} %all-reduce.4.cloned.1.call-done) | copy-start | bytes 3981316
  128.6 1.4 copy-start.4
  182.5 12.6 %copy-start.2 = (f32[2,2,12,1,6,512]{5,1,4,2,0,3:T(2,128)S(1)}, f32[2,2,12,1,6,512]{5,1,4,2,0,3:T(2,128)}, u32[]{:S(2)}) copy-start(f32[2,2,12,1,6,512]{5,1,4,2,0,3:T(2,128)} %copy.62) | copy-start | bytes 1769476
  182.5 18.5 %copy-start.7 = (f32[2,12,6,512]{3,0,2,1:T(2,128)S(1)}, f32[2,12,6,512]{3,0,2,1:T(2,128)}, u32[]{:S(2)}) copy-start(f32[2,12,6,512]{3,0,2,1:T(2,128)} %param.8) | copy-start | bytes 884740
  195.4 145.0 %copy-start.9 = (s32[10368]{0:T(1024)S(1)}, s32[10368]{0:T(1024)}, u32[]{:S(2)}) copy-start(s32[10368]{0:T(1024)} %copy-done.8) | copy-start | bytes 124420
  196.4 4.6 %collective-permute-start.9 = (f32[2,12,3,512]{3,0,2,1:T(2,128)S(1)}, f32[2,12,3,512]{3,0,2,1:T(2,128)S(1)}, u32[]{:S(2)}, u32[]{:S(2)}) collective-permute-start(f32[2,12,3,512]{3,0,2,1:T(2,128)S(1)} %get-tuple-element.15), channel_id=1, source_target_pairs={{0,1},{1,2},{2,3},{3,0},{4,5},{5,6},{6,7},{7,4},{8,9},{9,10},{10,1... | collective-permute-start | bytes 442376 | tf_op jit(solution)/shard_map/ppermute | solution.py:16
  340.4 29.4 %copy-start.11 = (s32[10368]{0:T(1024)S(1)}, s32[10368]{0:T(1024)}, u32[]{:S(2)}) copy-start(s32[10368]{0:T(1024)} %copy-done.10) | copy-start | bytes 124420
  369.9 29.9 %copy-start.1 = (f32[512,512]{1,0:T(8,128)S(1)}, f32[512,512]{1,0:T(8,128)}, u32[]{:S(2)}) copy-start(f32[512,512]{1,0:T(8,128)} %param.13) | copy-start | bytes 3145732
Sparse Core Ops, SparseCore 0:
  65.4 55.9 all-reduce.3
  182.6 150.9 all-reduce.5
where the time goes:
time: 413 us; the launch traced here: 407 us
  matrix products  171 us (41%)
  waiting for transfers between devices  149 us (36%)
  local copies, waits for them, and re-layouts  35.1 us (8%)
  starting transfers between devices  22.2 us (5%)
  other arithmetic  14.9 us (4%)
  between operations  14.7 us (4%)
    psum x1, waiting for transfers between devices, body(): lax.psum((grad_in_part, grad_out_part, score_sum), ('lat', 'lon'))  132 us
    dot_general x2, matrix products, sector_scatter(): lax.dot_general(flat_scores[:, level], one_hot, (((1,), (1,)), ((), ())),...  59.3 us
    dot_general x2, matrix products, sector_lookup(): jnp.dot(jnp.transpose(local_table), one_hot, precision=highest)  43.2 us
    ppermute x3, starting transfers between devices, extended(): lax.ppermute(lax.slice_in_dim(block, block.shape[dim] - width, None, axis...  15.1 us
    dot_general x1, matrix products, window_pass(): jnp.einsum('wtc,wtf->cf', normed * owned[..., None], grad_projected, prec...  12.9 us
    dot_general x1, matrix products, window_pass(): jnp.einsum('wtf,cf->wtc', grad_projected, in_weight, precision=highest)  12.6 us
  transfers between devices with their start and end apart: 12, of which 5 were waited for; matrix products, arithmetic and copies ran while one was open for 22% of the time, Pallas kernels for 0%

commit v1 on v0

v1 whole, which is shorter than its diff:
```python
import jax
import jax.numpy as jnp
from jax import lax
from jax.sharding import PartitionSpec as P

WIDTH = 512
HEADS = 16
HEAD_DIM = 32
WIN_LAT = 12
WIN_LON = 6


def shifted(value, axis, steps):
    count = lax.axis_size(axis)
    pairs = [(source, (source + steps) % count) for source in range(count)]
    return lax.ppermute(value, axis, pairs)


def split_windows(array):
    level_count, row_count, col_count = array.shape[:3]
    trailing = array.shape[3:]
    blocked = array.reshape(
        (level_count, row_count // WIN_LAT, WIN_LAT, col_count // WIN_LON, WIN_LON) + trailing
    )
    axis_order = (1, 3, 0, 2, 4) + tuple(range(5, 5 + len(trailing)))
    blocked = jnp.transpose(blocked, axis_order)
    return blocked.reshape(
        (row_count // WIN_LAT * (col_count // WIN_LON), level_count * WIN_LAT * WIN_LON) + trailing
    )


def join_windows(windows, level_count, row_count, col_count):
    trailing = windows.shape[2:]
    blocked = windows.reshape(
        (row_count // WIN_LAT, col_count // WIN_LON, level_count, WIN_LAT, WIN_LON) + trailing
    )
    axis_order = (2, 0, 3, 1, 4) + tuple(range(5, 5 + len(trailing)))
    blocked = jnp.transpose(blocked, axis_order)
    return blocked.reshape((level_count, row_count, col_count) + trailing)


def window_pass(inputs, cotangent, labels, in_weight, out_weight, bias_full):
    highest = lax.Precision.HIGH
    average = jnp.mean(inputs, axis=-1, keepdims=True)
    centered = inputs - average
    variance = jnp.mean(centered * centered, axis=-1, keepdims=True)
    inv_std = lax.rsqrt(variance + 1e-05)
    normed = centered * inv_std
    projected = jnp.einsum("wtc,cf->wtf", normed, in_weight, precision=highest)
    win_count, tok_count = (inputs.shape[0], inputs.shape[1])
    heads_split = projected.reshape(win_count, tok_count, 3, HEADS, HEAD_DIM)
    queries = heads_split[:, :, 0]
    key_vecs = heads_split[:, :, 1]
    value_vecs = heads_split[:, :, 2]
    factor = HEAD_DIM ** (-0.5)
    scores = (
        jnp.einsum("wqhd,wkhd->whqk", queries, key_vecs, precision=highest) * factor
        + bias_full[None]
    )
    allowed = (labels[:, :, None] == labels[:, None, :]) & (labels[:, None, :] > 0.5)
    scores = jnp.where(allowed[:, None], scores, -1000000000.0)
    peak = jnp.max(scores, axis=-1, keepdims=True)
    exponent = jnp.exp(scores - peak)
    probs = exponent / jnp.sum(exponent, axis=-1, keepdims=True)
    attended = jnp.einsum("whqk,wkhd->wqhd", probs, value_vecs, precision=highest).reshape(
        win_count, tok_count, WIDTH
    )
    grad_attended = jnp.einsum("wte,ce->wtc", cotangent, out_weight, precision=highest)
    grad_out_part = jnp.einsum(
        "wtc,wte->ce", attended, cotangent, precision=highest
    )
    grad_heads = grad_attended.reshape(win_count, tok_count, HEADS, HEAD_DIM)
    grad_probs = jnp.einsum("wqhd,wkhd->whqk", grad_heads, value_vecs, precision=highest)
    grad_values = jnp.einsum("whqk,wqhd->wkhd", probs, grad_heads, precision=highest)
    grad_scores = probs * (grad_probs - jnp.sum(grad_probs * probs, axis=-1, keepdims=True))
    grad_queries = jnp.einsum("whqk,wkhd->wqhd", grad_scores, key_vecs, precision=highest) * factor
    grad_keys = jnp.einsum("whqk,wqhd->wkhd", grad_scores, queries, precision=highest) * factor
    score_sum = jnp.sum(grad_scores, axis=0)
    grad_projected = jnp.stack([grad_queries, grad_keys, grad_values], axis=2).reshape(
        win_count, tok_count, 3 * WIDTH
    )
    grad_in_part = jnp.einsum(
        "wtc,wtf->cf", normed, grad_projected, precision=highest
    )
    grad_normed = jnp.einsum("wtf,cf->wtc", grad_projected, in_weight, precision=highest)
    grad_inputs = inv_std * (
        grad_normed
        - jnp.mean(grad_normed, axis=-1, keepdims=True)
        - normed * jnp.mean(grad_normed * normed, axis=-1, keepdims=True)
    )
    return (grad_inputs, grad_in_part, grad_out_part, score_sum)


def rounded(value):
    return lax.reduce_precision(value, exponent_bits=8, mantissa_bits=7)


def three_terms(value, axis):
    first = rounded(value)
    second = rounded(value - first)
    third = rounded(value - first - second)
    return jnp.concatenate([first, second, third], axis=axis).astype(jnp.bfloat16)


def body(fields, grad_out, region_ids, bias_index, bias_table, in_weight, out_weight):
    level_count, row_count, col_count, width = fields.shape
    half_rows = WIN_LAT // 2
    half_cols = WIN_LON // 2
    token_count = bias_index.shape[0]
    table_rows, head_count = bias_table.shape
    lon_count = lax.axis_size("lon")
    device_count = lon_count * lax.axis_size("lat")
    device = lax.axis_index("lat") * lon_count + lax.axis_index("lon")
    pair_count = token_count * token_count // device_count
    own_index = lax.dynamic_slice_in_dim(
        bias_index.reshape(-1), device * pair_count, pair_count, 0
    )
    one_hot = (
        own_index[:, None] == jnp.arange(table_rows, dtype=jnp.int32)[None, :]
    ).astype(jnp.bfloat16)
    found = lax.dot_general(
        three_terms(bias_table, 1), one_hot, (((0,), (1,)), ((), ())),
        preferred_element_type=jnp.float32,
    )
    found = found[:head_count] + found[head_count : 2 * head_count] + found[2 * head_count :]
    gathered = lax.all_gather(found, ("lat", "lon"), axis=0)
    bias_full = jnp.transpose(gathered, (1, 0, 2)).reshape(head_count, token_count, token_count)

    labels = (region_ids + 1).astype(jnp.float32)
    label_lanes = jnp.broadcast_to(labels[..., None], labels.shape + (128,))
    block = jnp.concatenate([fields, grad_out, label_lanes], axis=3)
    block = jnp.concatenate(
        [block[:, :, half_cols:], shifted(block[:, :, :half_cols], "lon", -1)], axis=2
    )
    block = jnp.concatenate(
        [shifted(block[:, row_count - half_rows :], "lat", 1), block[:, : row_count - half_rows]],
        axis=1,
    )
    frame_in = block[..., :width]
    frame_grad = block[..., width : 2 * width]
    wrapped = (lax.axis_index("lat") == 0) & (jnp.arange(row_count) < half_rows)
    frame_labels = block[..., 2 * width] + jnp.where(wrapped, 3.0, 0.0)[None, :, None]
    grad_win, grad_in_part, grad_out_part, score_sum = window_pass(
        split_windows(frame_in),
        split_windows(frame_grad),
        split_windows(frame_labels),
        in_weight,
        out_weight,
        bias_full,
    )
    own_scores = lax.psum_scatter(
        jnp.transpose(score_sum.reshape(head_count, device_count, pair_count), (1, 0, 2)),
        ("lat", "lon"), scatter_dimension=0, tiled=True,
    )[0]
    found = jnp.dot(three_terms(own_scores, 0), one_hot, preferred_element_type=jnp.float32)
    found = found[:head_count] + found[head_count : 2 * head_count] + found[2 * head_count :]
    grad_bias = lax.psum(
        lax.psum_scatter(jnp.transpose(found), "lon", scatter_dimension=0, tiled=True), "lat"
    )
    weights_part = jnp.concatenate([grad_in_part, grad_out_part], axis=1)
    weights = lax.psum(
        lax.psum_scatter(weights_part, "lon", scatter_dimension=0, tiled=True), "lat"
    )
    grad_frame = join_windows(grad_win, level_count, row_count, col_count)
    grad_frame = jnp.concatenate(
        [grad_frame[:, half_rows:], shifted(grad_frame[:, :half_rows], "lat", -1)], axis=1
    )
    grad_frame = jnp.concatenate(
        [
            shifted(grad_frame[:, :, col_count - half_cols :], "lon", 1),
            grad_frame[:, :, : col_count - half_cols],
        ],
        axis=2,
    )
    return (grad_out + grad_frame, weights[:, : 3 * width], weights[:, 3 * width :], grad_bias)


def solution(mesh):
    in_specs = (
        P(None, "lat", "lon", None),
        P(None, "lat", "lon", None),
        P(None, "lat", "lon"),
        P(),
        P(),
        P(),
        P(),
    )
    out_specs = (P(None, "lat", "lon", None), P("lon", None), P("lon", None), P("lon", None))
    return jax.shard_map(body, mesh=mesh, in_specs=in_specs, out_specs=out_specs, check_vma=False)
```

time: 413 us -> 383 us (0.927); the launches traced: 407 us -> 382 us
  matrix products: 171 us -> 34.9 us
  waiting for transfers between devices: 149 us -> 276 us
  starting transfers between devices: 22.2 us -> 9 us
  other arithmetic: 14.9 us -> 10.1 us
    reduce_scatter x0 -> x2, waiting for transfers between devices: none -> 130 us  [the longest x1 84.7 us: body(): lax.psum_scatter(jnp.transpose(score_sum.reshape(head_count, device_count...]
    dot_general x6 -> x4, matrix products: 120 us -> 10.8 us  [the longest x1 3.27 us: body(): lax.dot_general(three_terms(bias_table, 1), one_hot, (((0,), (1,)), ((),...]
    psum x2 -> x1, waiting for transfers between devices: 140 us -> 69.1 us  [body(): lax.psum(lax.psum_scatter(weights_part, 'lon', scatter_dimension=0, tiled...]
    all_gather x0 -> x1, waiting for transfers between devices: none -> 35.2 us  [body(): gathered = lax.all_gather(found, ('lat', 'lon'), axis=0)]
    unnamed x2 -> x6, waiting for transfers between devices: 0.03 us -> 24.2 us
    ppermute x6 -> x0, starting transfers between devices: 19 us -> none  [the longest x3 15.1 us: extended(): lax.ppermute(lax.slice_in_dim(block, block.shape[dim] - width, None, axis...]
    ppermute x4, waiting for transfers between devices: 5.77 us -> 17.5 us  [shifted(): return lax.ppermute(value, axis, pairs)]
    unnamed x25 -> x39, local copies, waits for them, and re-layouts: 4.93 us -> 13.9 us
  transfers between devices with their start and end apart: 12 -> 9, of which waited for: 5 -> 9; matrix products, arithmetic and copies ran while one was open for 22% -> 11% of each run, Pallas kernels for 0% -> 0%
where the time goes in v1:
time: 383 us; the launch traced here: 382 us
  waiting for transfers between devices  276 us (72%)
  local copies, waits for them, and re-layouts  38.3 us (10%)
  matrix products  34.9 us (9%)
  between operations  14.2 us (4%)
  other arithmetic  10.1 us (3%)
  starting transfers between devices  9 us (2%)
    reduce_scatter x1, waiting for transfers between devices, body(): lax.psum_scatter(jnp.transpose(score_sum.reshape(head_count, device_count...  84.7 us
    psum x1, waiting for transfers between devices, body(): lax.psum(lax.psum_scatter(weights_part, 'lon', scatter_dimension=0, tiled...  69.1 us
    reduce_scatter x1, waiting for transfers between devices, body(): lax.psum_scatter(weights_part, 'lon', scatter_dimension=0, tiled=True)  45 us
    all_gather x1, waiting for transfers between devices, body(): gathered = lax.all_gather(found, ('lat', 'lon'), axis=0)  35.2 us
    unnamed x6, waiting for transfers between devices  24.2 us
    ppermute x4, waiting for transfers between devices, shifted(): return lax.ppermute(value, axis, pairs)  17.5 us
    unnamed x39, local copies, waits for them, and re-layouts  13.9 us
    ppermute x4, starting transfers between devices, shifted(): return lax.ppermute(value, axis, pairs)  8.35 us
  transfers between devices with their start and end apart: 9, of which 9 were waited for; matrix products, arithmetic and copies ran while one was open for 11% of the time, Pallas kernels for 0%

profile of v1, /device:TPU:0, one launch (start us, length us, event | category | flops | bytes accessed | tf_op | source)
XLA Modules:
  0.0 382.3 jit_solution(1877611293819735499)
XLA Ops:
  9.8 2.4 collective-permute-start
  12.5 3.3 fusion.1
  19.6 3.5 copy.65
  23.1 7.2 %collective-permute-done.1 = f32[2,6,6,1152]{3,0,2,1:T(2,128)S(1)} collective-permute-done((f32[2,6,6,1152]{3,0,2,1:T(2,128)S(1)}, f32[2,6,6,1152]{3,0,2,1:T(2,128)S(1)}, u32[]{:S(2)}, u32[]{:S(2)}) %collective-permute-start.1) | collective-permute-done | bytes 331808 | tf_op jit(solution)/shard_map/ppermute | solution.py:16
  33.5 4.6 %convolution_bitcast_fusion = f32[1,144,3,16,32]{1,4,3,2,0:T(8,128)} fusion(f32[3,16,32,512]{3,2,1,0:T(8,128)} %bitcast.89, f32[1,144,1,1,1,1,512]{6,1,5,4,3,2,0:T(8,128)S(1)} %reshape_transpose_reshape.9, f32[144]{0:T(256)S(1)} %rsqrt.12, f32[144]{0:T(256)S(1)} %div.25), kind=kOutput, calls=%fused_computation.14 | convolution fusion | flops 679624704 | bytes 4326528 | tf_op jit(solution)/shard_map/wtc,cf->wtf/dot_general | solution.py:49
  39.6 35.2 %all-gather.3.cloned.1.call-done = f32[512,648]{1,0:T(8,128)} async-done(((f32[16,648]{1,0:T(8,128)}), f32[512,648]{1,0:T(8,128)}) %all-gather.3.cloned.1.call-update) | async-done | bytes 1327120 | tf_op jit(solution)/shard_map/all_gather | solution.py:126
  77.1 3.2 broadcast_in_dim_reshape.3
  80.2 2.4 copy.68
  82.7 2.7 fusion.44
  86.9 2.6 multiply_reduce_fusion
  92.4 3.1 reshape.375
  95.6 3.5 copy.78
  100.9 3.2 fusion.6
  110.5 84.7 %reduce-scatter.8.cloned.1.call-done = f32[1,16,648]{2,1,0:T(8,128)} async-done(((f32[32,16,648]{2,1,0:T(8,128)}), f32[1,16,648]{2,1,0:T(8,128)}) %reduce-scatter.8.cloned.1.call-update) | async-done | bytes 41488 | tf_op jit(solution)/shard_map/reduce_scatter | solution.py:151
  196.0 3.1 fusion
  203.9 2.8 fusion.23
  206.7 2.5 pad_maximum_fusion
  210.3 4.8 %fusion.41 = (f32[144]{0:T(256)S(1)}, f32[144]{0:T(256)S(1)}, f32[144,512]{1,0:T(8,128)S(1)}) fusion(f32[144]{0:T(256)S(1)} %rsqrt.12, f32[144,512]{1,0:T(8,128)S(1)} %reshape_transpose_reshape.10, f32[144]{0:T(256)S(1)} %div.25, f32[144,1536]{0,1:T(8,128)S(1)} %bitcast.88, f32[512,1536]{1,0:T(8,128)} %param.12), kind=kOutput, calls=%fused_computation.89 | convolution fusion | flops 679845632 | bytes 4622592 | tf_op jit(solution)/shard_map/wtf,cf->wtc/dot_general | solution.py:85
  215.1 24.1 %reduce-scatter.10.cloned.1.call-done = f32[1584,16]{1,0:T(8,128)} async-done(((f32[6336,16]{1,0:T(8,128)}), f32[1584,16]{1,0:T(8,128)}) %reduce-scatter.10.cloned.1.call-update) | async-done | bytes 101392
  241.3 45.0 %reduce-scatter.6.cloned.1.call-done = f32[128,2048]{1,0:T(8,128)} async-done(((f32[512,2048]{1,0:T(8,128)}), f32[128,2048]{1,0:T(8,128)}) %reduce-scatter.6.cloned.1.call-update) | async-done | bytes 1048592 | tf_op jit(solution)/shard_map/reduce_scatter | solution.py:162
  286.6 4.3 %collective-permute-start.2 = (f32[2,6,6,512]{3,2,1,0:T(8,128)S(1)}, f32[2,6,6,512]{3,2,1,0:T(8,128)S(1)}, u32[]{:S(2)}, u32[]{:S(2)}) collective-permute-start(f32[2,6,6,512]{3,2,1,0:T(8,128)S(1)} %get-tuple-element.30), channel_id=1, source_target_pairs={{0,28},{4,0},{8,4},{12,8},{16,12},{20,16},{24,20},{28,24},{1,29},{... | collective-permute-start | bytes 442376 | tf_op jit(solution)/shard_map/ppermute | solution.py:16
  290.9 4.1 %collective-permute-done.2 = f32[2,6,6,512]{3,2,1,0:T(8,128)S(1)} collective-permute-done((f32[2,6,6,512]{3,2,1,0:T(8,128)S(1)}, f32[2,6,6,512]{3,2,1,0:T(8,128)S(1)}, u32[]{:S(2)}, u32[]{:S(2)}) %collective-permute-start.2) | collective-permute-done | bytes 147488 | tf_op jit(solution)/shard_map/ppermute | solution.py:16
  295.2 5.1 %collective-permute-done.3 = f32[2,12,3,512]{3,2,1,0:T(4,128)S(1)} collective-permute-done((f32[2,12,3,512]{3,2,1,0:T(4,128)S(1)}, f32[2,12,3,512]{3,2,1,0:T(4,128)S(1)}, u32[]{:S(2)}, u32[]{:S(2)}) %collective-permute-start.3) | collective-permute-done | bytes 147488 | tf_op jit(solution)/shard_map/ppermute | solution.py:16
  301.4 69.1 %all-reduce.3.cloned.1.call-done = (f32[128,2048]{1,0:T(8,128)}, f32[1584,16]{0,1:T(8,128)}) async-done(((f32[128,2048]{1,0:T(8,128)}, f32[1584,16]{0,1:T(8,128)}), (f32[128,2048]{1,0:T(8,128)}, f32[1584,16]{0,1:T(8,128)})) %all-reduce.3.cloned.1.call-update) | async-done | bytes 1149968 | tf_op jit(solution)/shard_map/psum | solution.py:161
  (105 shorter events, 41.3 us)
Async XLA Ops:
  7.2 31.0 %copy-start = (f32[512,512]{1,0:T(8,128)S(1)}, f32[512,512]{1,0:T(8,128)}, u32[]{:S(2)}) copy-start(f32[512,512]{1,0:T(8,128)} %param.13) | copy-start | bytes 3145732
  7.2 5.0 %copy-start.15 = (f32[6336,16]{0,1:T(8,128)S(1)}, f32[6336,16]{0,1:T(8,128)}, u32[]{:S(2)}) copy-start(f32[6336,16]{0,1:T(8,128)} %param.11) | copy-start | bytes 1216516
  7.2 5.1 %copy-start.16 = (s32[144,144]{1,0:T(8,128)S(1)}, s32[144,144]{1,0:T(8,128)}, u32[]{:S(2)}) copy-start(s32[144,144]{1,0:T(8,128)} %param.10) | copy-start | bytes 248836
  7.2 67.6 %all-gather.3.cloned.1.call-start = ((), (), s32[]{:S(2)}) async-start(), calls=%async_computation.5 | async-start | bytes 1622016 | tf_op jit(solution)/shard_map/all_gather | solution.py:126
  9.8 7.1 %collective-permute-start = (f32[2,12,3,1152]{3,0,2,1:T(2,128)S(1)}, f32[2,12,3,1152]{3,0,2,1:T(2,128)S(1)}, u32[]{:S(2)}, u32[]{:S(2)}) collective-permute-start(f32[2,12,3,1152]{3,0,2,1:T(2,128)S(1)} %get-tuple-element.24), channel_id=1, source_target_pairs={{0,3},{1,0},{2,1},{3,2},{4,7},{5,4},{6,5},{7,6},{8,11},{9,8},{10,9... | collective-permute-start | bytes 995336 | tf_op jit(solution)/shard_map/ppermute | solution.py:16
  17.0 13.4 %collective-permute-start.1 = (f32[2,6,6,1152]{3,0,2,1:T(2,128)S(1)}, f32[2,6,6,1152]{3,0,2,1:T(2,128)S(1)}, u32[]{:S(2)}, u32[]{:S(2)}) collective-permute-start(f32[2,6,6,1152]{3,0,2,1:T(2,128)S(1)} %fusion.21), channel_id=1, source_target_pairs={{0,4},{4,8},{8,12},{12,16},{16,20},{20,24},{24,28},{28,0},{1,5},{5... | collective-permute-start | bytes 995336 | tf_op jit(solution)/shard_map/ppermute | solution.py:16
  19.2 176.0 %reduce-scatter.8.cloned.1.call-start = ((), (), s32[]{:S(2)}) async-start(), calls=%async_computation.4 | async-start | bytes 1622016 | tf_op jit(solution)/shard_map/reduce_scatter | solution.py:151
  33.3 4.8 %copy-start.5 = (f32[2,12,6,512]{3,2,1,0:T(8,128)}, f32[2,12,6,512]{3,2,1,0:T(8,128)S(1)}, u32[]{:S(2)}) copy-start(f32[2,12,6,512]{3,2,1,0:T(8,128)S(1)} %copy.63) | copy-start | bytes 884740
  33.4 4.8 %copy-start.8 = (f32[1,144,1,1,1,1,512]{6,1,5,4,3,2,0:T(8,128)}, f32[1,144,1,1,1,1,512]{6,1,5,4,3,2,0:T(8,128)S(1)}, u32[]{:S(2)}) copy-start(f32[1,144,1,1,1,1,512]{6,1,5,4,3,2,0:T(8,128)S(1)} %reshape_transpose_reshape.9) | copy-start | bytes 884740
  85.4 4.1 %copy-start.1 = (f32[16,144,144]{1,2,0:T(8,128)}, f32[16,144,144]{1,2,0:T(8,128)S(1)}, u32[]{:S(2)}) copy-start(f32[16,144,144]{1,2,0:T(8,128)S(1)} %get-tuple-element.35) | copy-start | bytes 3981316
  85.5 1.4 copy-start.13
  99.1 140.2 %reduce-scatter.10.cloned.1.call-start = ((), (), s32[]{:S(2)}) async-start(), calls=%async_computation.6 | async-start | bytes 4055040
  100.9 3.2 copy-start.3
  104.1 1.7 copy-start.2
  105.8 2.5 copy-start.14
  201.5 1.0 copy-start.10
  201.5 2.4 copy-start.9
  201.6 84.8 %reduce-scatter.6.cloned.1.call-start = ((), (), s32[]{:S(2)}) async-start(), calls=%async_computation.3 | async-start | bytes 5242880 | tf_op jit(solution)/shard_map/reduce_scatter | solution.py:162
  203.9 2.8 copy-start.4
  209.2 1.0 copy-start.6
  209.2 161.2 %all-reduce.3.cloned.1.call-start = ((), (), s32[]{:S(2)}) async-start(), calls=%async_computation.7 | async-start | bytes 2310144 | tf_op jit(solution)/shard_map/psum | solution.py:161
  215.1 85.2 %copy-start.11 = (f32[2,12,6,512]{3,0,2,1:T(2,128)S(1)}, f32[2,12,6,512]{3,0,2,1:T(2,128)}, u32[]{:S(2)}) copy-start(f32[2,12,6,512]{3,0,2,1:T(2,128)} %param.8) | copy-start | bytes 884740
  286.6 8.4 %collective-permute-start.2 = (f32[2,6,6,512]{3,2,1,0:T(8,128)S(1)}, f32[2,6,6,512]{3,2,1,0:T(8,128)S(1)}, u32[]{:S(2)}, u32[]{:S(2)}) collective-permute-start(f32[2,6,6,512]{3,2,1,0:T(8,128)S(1)} %get-tuple-element.30), channel_id=1, source_target_pairs={{0,28},{4,0},{8,4},{12,8},{16,12},{20,16},{24,20},{28,24},{1,29},{... | collective-permute-start | bytes 442376 | tf_op jit(solution)/shard_map/ppermute | solution.py:16
  295.1 5.1 %collective-permute-start.3 = (f32[2,12,3,512]{3,2,1,0:T(4,128)S(1)}, f32[2,12,3,512]{3,2,1,0:T(4,128)S(1)}, u32[]{:S(2)}, u32[]{:S(2)}) collective-permute-start(f32[2,12,3,512]{3,2,1,0:T(4,128)S(1)} %fusion.25), channel_id=1, source_target_pairs={{0,1},{1,2},{2,3},{3,0},{4,5},{5,6},{6,7},{7,4},{8,9},{9,10},{10,1... | collective-permute-start | bytes 442376 | tf_op jit(solution)/shard_map/ppermute | solution.py:16
  (2 other events, 1.8 us)
Sparse Core Ops, SparseCore 0:
  19.3 55.3 all-gather.2
  99.2 95.9 reduce-scatter.7
  201.7 37.5 reduce-scatter.9
  241.8 44.5 reduce-scatter.5
  290.3 80.1 all-reduce.2
